TPU v7x, 32 devices: a whole 2x2x4 slice. The times are simulated.
32 devices in a mesh: dp: 2 (over y), blk: 4 (over z), uly: 4 (over x, core).
Axes of the slice: x: 2, y: 2, z: 4, core: 2. Of those that a mesh axis runs over, the one named last changes fastest.
Arguments:
- hidden_states: bfloat16 [2, 4096, 4096], P('dp', ('blk', 'uly')), may hold values from -96 to 96
- block_table: int32 [2, 8, 8], P('dp'), may hold values from 0 to 1, as said below
- w_query: bfloat16 [4096, 2048], P(('dp', 'blk'), 'uly'), may hold values from -0.09375 to 0.09375
- w_key: bfloat16 [4096, 512], P(('dp', 'blk'), 'uly'), may hold values from -0.09375 to 0.09375
- w_value: bfloat16 [4096, 512], P(('dp', 'blk'), 'uly'), may hold values from -0.09375 to 0.09375
Outputs:
- attended: bfloat16 [2, 4096, 2048], P('dp', ('blk', 'uly'))
Inputs may be any that keep to these rules, and one draw needn't show every extreme that they name: block_table[s, i, j] is 1 where query block i of sequence s may read key block j, else 0; it is 1 on the diagonal and 0 above it; below the diagonal a block is allowed when it lies within a window of 1 to 4 blocks ending at i, or is one of the sequence's global key blocks; the global key blocks are block 0 and exactly 2 others.
All inputs are finite; a program needn't handle non-finite values.
Results may differ from a plain program's by a relative error of at most 0.024.
The roundings to bfloat16 on the way count: a program that leaves them out, or rounds other values in their place, can miss the bound.
Values may be sent and summed in bfloat16 or wider, within the bound.
A program may use at most 128 MiB of HBM per device.

v0:
```python
import functools

import jax
import jax.numpy as jnp
from jax import lax
from jax.experimental import pallas as pl
from jax.experimental.pallas import tpu as pltpu
from jax.sharding import PartitionSpec as P

H = 16
KV = 4
HD = 128
MBLK = 512
THETA_BASE = 500000.0
LOG2E = 1.4426950408889634
NT = (((1,), (1,)), ((), ()))
TN = (((0,), (0,)), ((), ()))


def from_partner(array, axis, distance):
    return lax.ppermute(array, axis, [(i, i ^ 1 << distance) for i in range(lax.axis_size(axis))])


def angle_tables(positions):
    half_dim = HD // 2
    exponent = jnp.arange(half_dim, dtype=jnp.float32) * (2.0 / HD)
    frequency = jnp.power(jnp.float32(THETA_BASE), -exponent)
    angles = positions.astype(jnp.float32)[:, None] * frequency[None, :]
    return jnp.cos(angles), jnp.sin(angles)


def rotate(values, cosine, sine):
    cosine, sine = cosine[:, None, :], sine[:, None, :]
    half_dim = HD // 2
    first, second = values[..., :half_dim], values[..., half_dim:]
    return jnp.concatenate([first * cosine - second * sine, second * cosine + first * sine], axis=-1)


def attend_kernel(heads, tiles, table, rank, q_ref, kv_ref, out_ref, best, total, accum):
    scale = HD**-0.5 * LOG2E

    def visit(q_start, key_block, diagonal):
        k_start = pl.multiple_of(key_block * MBLK, MBLK)
        key = kv_ref[pl.ds(k_start, MBLK), :HD]
        value = kv_ref[pl.ds(k_start, MBLK), HD:]
        for head in range(heads):
            cols = pl.ds(head * MBLK, MBLK)
            query = q_ref[pl.ds(q_start, MBLK), head * HD : (head + 1) * HD]
            scores = lax.dot_general(key, query, NT, preferred_element_type=jnp.float32) * scale
            if diagonal:
                key_at = lax.broadcasted_iota(jnp.int32, (MBLK, MBLK), 0)
                query_at = lax.broadcasted_iota(jnp.int32, (MBLK, MBLK), 1)
                scores = jnp.where(key_at <= query_at, scores, -1e30)
                new_best = jnp.max(scores, axis=0, keepdims=True)
            else:
                old_best = best[:, cols]
                new_best = jnp.maximum(old_best, jnp.max(scores, axis=0, keepdims=True))
            weights = jnp.exp2(scores - new_best)
            sums = jnp.sum(weights, axis=0, keepdims=True)
            mixed = lax.dot_general(
                value, weights.astype(jnp.bfloat16), TN, preferred_element_type=jnp.float32
            )
            best[:, cols] = new_best
            if diagonal:
                total[:, cols] = sums
                accum[:, cols] = mixed
            else:
                rescale = jnp.exp2(old_best - new_best)
                total[:, cols] = total[:, cols] * rescale + sums
                accum[:, cols] = accum[:, cols] * rescale + mixed

    for tile in range(tiles):
        q_start = tile * MBLK
        block = rank[0] * tiles + tile
        visit(q_start, block, True)

        @pl.loop(0, block)
        def _(key_block, q_start=q_start, block=block):
            @pl.when(table[block, key_block] > 0)
            def _():
                visit(q_start, key_block, False)

        for head in range(heads):
            cols = pl.ds(head * MBLK, MBLK)
            final = accum[:, cols] / total[:, cols]
            out_ref[pl.ds(q_start, MBLK), head * HD : (head + 1) * HD] = final.T.astype(jnp.bfloat16)


def attend(table, rank, query, key_value, heads, tiles):
    rows = query.shape[0]
    smem = pl.BlockSpec(memory_space=pltpu.SMEM)
    vmem = pl.BlockSpec(memory_space=pltpu.VMEM)
    return pl.pallas_call(
        functools.partial(attend_kernel, heads, tiles),
        out_shape=jax.ShapeDtypeStruct((rows, heads * HD), jnp.bfloat16),
        in_specs=[smem, smem, vmem, vmem],
        out_specs=vmem,
        scratch_shapes=[
            pltpu.VMEM((1, heads * MBLK), jnp.float32),
            pltpu.VMEM((1, heads * MBLK), jnp.float32),
            pltpu.VMEM((HD, heads * MBLK), jnp.float32),
        ],
        compiler_params=pltpu.CompilerParams(vmem_limit_bytes=48 * 1024 * 1024),
        cost_estimate=pl.CostEstimate(flops=8 * 10**9, bytes_accessed=4 * 10**6, transcendentals=16 * 10**6),
    )(table, rank, query, key_value)


def shards(hidden_states, block_table, w_query, w_key, w_value):
    tokens = hidden_states.shape[1]
    uly_size = lax.axis_size("uly")
    uly_rank = lax.axis_index("uly")
    blk_rank = lax.axis_index("blk")
    heads_here = H // uly_size
    repeats = uly_size // KV
    part_cols = HD // repeats
    query_cols = heads_here * HD
    group_rows = tokens * uly_size
    tiles = group_rows // MBLK
    w_joined = jnp.concatenate([w_query, w_key, w_value], axis=1)
    w_rows = lax.all_gather(w_joined, ("dp", "blk"), axis=0, tiled=True)
    projected = jnp.dot(
        lax.all_gather(hidden_states[0], "uly", axis=0, tiled=True),
        w_rows,
        preferred_element_type=jnp.float32,
    )
    positions = blk_rank * group_rows + jnp.arange(group_rows, dtype=jnp.int32)
    cosine, sine = angle_tables(positions)
    query = rotate(projected[:, :query_cols].reshape(group_rows, heads_here, HD), cosine, sine)
    query = query.astype(jnp.bfloat16).reshape(group_rows, query_cols)
    pieces = jnp.stack(
        [projected[:, query_cols : query_cols + part_cols], projected[:, query_cols + part_cols :]]
    )
    part_index = uly_rank % repeats
    for bit_index in range(repeats.bit_length() - 1):
        partner_piece = from_partner(pieces, "uly", bit_index)
        upper_part = part_index >> bit_index & 1 == 1
        pieces = jnp.where(
            upper_part,
            jnp.concatenate([partner_piece, pieces], axis=-1),
            jnp.concatenate([pieces, partner_piece], axis=-1),
        )
    key = rotate(pieces[0][:, None, :], cosine, sine)[:, 0, :].astype(jnp.bfloat16)
    key_value = jnp.concatenate([key, pieces[1].astype(jnp.bfloat16)], axis=1)
    key_value = lax.all_gather(key_value, "blk", axis=0, tiled=True)
    result = attend(
        block_table[0], blk_rank[None].astype(jnp.int32), query, key_value, heads_here, tiles
    )
    merged = lax.all_to_all(result, "uly", split_axis=0, concat_axis=1, tiled=True)
    return merged[None]


def solution(mesh):
    placed = (
        P("dp", ("blk", "uly"), None),
        P("dp", None, None),
        P(("dp", "blk"), "uly"),
        P(("dp", "blk"), "uly"),
        P(("dp", "blk"), "uly"),
    )
    return jax.shard_map(
        shards, mesh=mesh, in_specs=placed, out_specs=P("dp", ("blk", "uly"), None), check_vma=False
    )
```

profile of v0, /device:TPU:28, one launch (start us, length us, event | category | flops | bytes accessed | tf_op | source)
XLA Modules:
  0.0 276.1 jit_solution(10673429409730703340)
XLA Ops:
  6.5 2.1 pad_maximum_fusion.1
  8.7 0.0 all-gather.5.cloned.1.call-update
  8.7 0.0 all-gather.9.cloned.1.call-start
  8.7 0.7 all-gather.9.cloned.1.call-update
  9.4 0.0 all-gather.7.cloned.1.call-start
  9.5 97.1 %all-gather.5.cloned.1.call-done = bf16[4096,768]{1,0:T(8,128)(2,1)} async-done(((bf16[512,768]{1,0:T(8,128)(2,1)}), bf16[4096,768]{1,0:T(8,128)(2,1)}) %all-gather.5.cloned.1.call-update) | async-done | bytes 6291472 | tf_op jit(solution)/shard_map/all_gather | solution.py:120
  106.7 60.9 %all-gather.9.cloned.1.call-done = bf16[1,1024,4096]{2,1,0:T(8,128)(2,1)} async-done(((bf16[1,256,4096]{2,1,0:T(8,128)(2,1)}), bf16[1,1024,4096]{2,1,0:T(8,128)(2,1)}) %all-gather.9.cloned.1.call-update) | async-done | bytes 8388624 | tf_op jit(solution)/shard_map/all_gather | solution.py:122
  167.5 10.9 %fusion.2 = f32[1024,768]{1,0:T(8,128)S(1)} fusion(bf16[4096,768]{1,0:T(8,128)(2,1)} %all-gather.5.cloned.1.call-done, bf16[1,1024,4096]{2,1,0:T(8,128)(2,1)} %all-gather.9.cloned.1.call-done), kind=kOutput, calls=%fused_computation.4 | convolution fusion | flops 6442450944 | bytes 17825792 | tf_op jit(solution)/shard_map/dot_general | solution.py:121
  178.5 2.4 fusion.10
  180.9 0.1 maximum_bitcast_fusion
  181.1 0.9 pad_maximum_fusion.2
  181.9 0.0 all-gather.7.cloned.1.call-update
  182.0 3.0 %multiply_cosine_fusion.1 = (f32[1024,64]{1,0:T(8,128)}, f32[1024,64]{1,0:T(8,128)}) fusion(f32[64]{0:T(128)S(1)} %negate_power_fusion, f32[1024]{0:T(1024)S(1)} %add_convert_fusion.1), kind=kLoop, calls=%fused_computation.11 | loop fusion | flops 65536 | bytes 528640 | tf_op jit(solution)/shard_map/cos | solution.py:29
  185.0 1.6 slice.29
  186.7 2.0 reshape.115
  188.7 1.6 subtract_convert_fusion
  190.3 1.4 pad_maximum_fusion
  191.8 0.2 copy.14
  192.0 33.9 %all-gather.7.cloned.1.call-done.kv_ref = bf16[4096,256]{1,0:T(8,128)(2,1)} async-done(((bf16[1024,256]{1,0:T(8,128)(2,1)}), bf16[4096,256]{1,0:T(8,128)(2,1)}) %all-gather.7.cloned.1.call-update) | async-done | bytes 2097168 | tf_op jit(solution)/shard_map/all_gather | solution.py:144
  225.9 1.6 copy-done
  227.5 22.7 %shard_map.55 = bf16[1024,512]{1,0:T(8,128)(2,1)S(1)} custom-call(s32[8,8]{1,0:T(8,128)S(1)} %bitcast.22, s32[1]{0:T(128)} %bitcast.1.rank, bf16[1024,512]{1,0:T(8,128)(2,1)S(1)} %bitcast.20, bf16[4096,256]{1,0:T(8,128)(2,1)S(1)} %copy-done), custom_call_target="tpu_custom_call" | custom-call | flops 8000000000 | bytes 4000000 | tf_op jit(solution)/shard_map/pallas_call | solution.py:93
  250.2 17.0 %all_to_all.16 = bf16[4,256,512]{2,1,0:T(8,128)(2,1)S(1)} all-to-all(bf16[4,256,512]{2,1,0:T(8,128)(2,1)S(1)} %bitcast.21), channel_id=1, replica_groups=mesh['dp'=2,'blk'=4,'uly'=4] {'uly'}, dimensions={0} | all-to-all | bytes 2097152 | tf_op jit(solution)/shard_map/all_to_all | solution.py:148
  267.2 0.8 copy.10
  268.0 1.6 broadcast_in_dim.5
  (12 shorter events, 0.1 us)
Async XLA Ops:
  6.5 100.1 %all-gather.5.cloned.1.call-start = ((), (), s32[]{:S(2)}) async-start(), calls=%async_computation.1 | async-start | bytes 7077888 | tf_op jit(solution)/shard_map/all_gather | solution.py:120
  8.7 158.8 %all-gather.9.cloned.1.call-start = ((), (), s32[]{:S(2)}) async-start(), calls=%async_computation.3 | async-start | bytes 10485760 | tf_op jit(solution)/shard_map/all_gather | solution.py:122
  9.4 216.4 %all-gather.7.cloned.1.call-start = ((), (), s32[]{:S(2)}) async-start(), calls=%async_computation.2 | async-start | bytes 2621440 | tf_op jit(solution)/shard_map/all_gather | solution.py:144
  186.7 2.0 copy-start.2
  186.7 2.0 copy-start.3
  190.3 35.6 %copy-start.1 = (s32[1,8,8]{2,1,0:T(8,128)S(1)}, s32[1,8,8]{2,1,0:T(8,128)}, u32[]{:S(2)}) copy-start(s32[1,8,8]{2,1,0:T(8,128)} %param.6) | copy-start | bytes 772
  225.9 1.6 copy-start
Sparse Core Ops, SparseCore 0:
  9.4 97.1 all-gather.4
  108.2 59.2 all-gather.8
  182.1 43.7 all-gather.6
where the time goes:
time: 277 us; the launch traced here: 276 us
  waiting for transfers between devices  193 us (70%)
  Pallas kernels  22.7 us (8%)
  blocking collectives  17 us (6%)
  between operations  13.2 us (5%)
  other arithmetic  11.6 us (4%)
  matrix products  10.9 us (4%)
  local copies, waits for them, and re-layouts  7.92 us (3%)
    all_gather x1, waiting for transfers between devices, shards(): w_rows = lax.all_gather(w_joined, ('dp', 'blk'), axis=0, tiled=True)  97.1 us
    all_gather x1, waiting for transfers between devices, shards(): lax.all_gather(hidden_states[0], 'uly', axis=0, tiled=True)  60.9 us
    all_gather x1, waiting for transfers between devices, shards(): key_value = lax.all_gather(key_value, 'blk', axis=0, tiled=True)  33.9 us
    pallas_call x1, Pallas kernels, attend(): pl.pallas_call(functools.partial(attend_kernel, heads, tiles), out_shape=...  22.7 us
    all_to_all x1, blocking collectives, shards(): lax.all_to_all(result, 'uly', split_axis=0, concat_axis=1, tiled=True)  17 us
    dot_general x1, matrix products, shards(): jnp.dot(lax.all_gather(hidden_states[0], 'uly', axis=0, tiled=True), w_ro...  10.9 us
  transfers between devices with their start and end apart: 3, of which 3 were waited for; matrix products, arithmetic and copies ran while one was open for 4% of the time, Pallas kernels for 0%

commit v1 on v0

--- a/solution.py
+++ b/solution.py
@@ -105,6 +105,313 @@
     )(table, rank, query, key_value)
 
 
+PIECE = 256
+MESH = pl.DeviceIdType.MESH
+HIDDEN_STEPS = 6
+
+
+def project_kernel(
+    dp_n, blk_n, hid, wq, wk, wv, cos_ref, sin_ref, q_out, kv_out,
+    weights, rows_all, acc, kv, local_sem, w_send, w_recv, h_send, h_recv, kv_send, kv_recv,
+):
+    y, z, u = lax.axis_index("dp"), lax.axis_index("blk"), lax.axis_index("uly")
+    last = blk_n - 1
+    chunks = dp_n * blk_n
+    pieces = weights.shape[0]
+    tokens = hid.shape[0]
+    depth = wq.shape[0]
+    group = rows_all.shape[1]
+    up, down, across = {"blk": z + 1}, {"blk": z - 1}, {"dp": 1 - y}
+    core = u + 1 - 2 * (u % 2)
+    chip = (u + 2) % 4
+    far = (core + 2) % 4
+    mine = y * blk_n + z
+
+    barrier = pltpu.get_barrier_semaphore()
+
+    @pl.when(z < last)
+    def _():
+        pl.semaphore_signal(barrier, inc=1, device_id=up, device_id_type=MESH)
+
+    @pl.when(z > 0)
+    def _():
+        pl.semaphore_signal(barrier, inc=1, device_id=down, device_id_type=MESH)
+
+    for where in (across, {"uly": core}, {"uly": chip}):
+        pl.semaphore_signal(barrier, inc=1, device_id=where, device_id_type=MESH)
+
+    own = [
+        pltpu.make_async_copy(wk, weights.at[0, mine, :, pl.ds(0, HD)], local_sem.at[0]),
+        pltpu.make_async_copy(wv, weights.at[0, mine, :, pl.ds(HD, HD)], local_sem.at[1]),
+    ]
+    for p in range(1, pieces):
+        own.append(
+            pltpu.make_async_copy(
+                wq.at[:, pl.ds((p - 1) * PIECE, PIECE)], weights.at[p, mine], local_sem.at[p + 1]
+            )
+        )
+    for c in range(chunks):
+        own.append(
+            pltpu.make_async_copy(
+                hid.at[:, pl.ds(c * depth, depth)],
+                rows_all.at[c, pl.ds(u * tokens, tokens)],
+                local_sem.at[pieces + 1 + c],
+            )
+        )
+    for copy in own:
+        copy.start()
+    middle = jnp.where((z > 0) & (z < last), 1, 0)
+    pl.semaphore_wait(barrier, 4 + middle)
+
+    def weight_copy(p, way, source_z, where, rank):
+        return pltpu.make_async_remote_copy(
+            src_ref=weights.at[p, rank], dst_ref=weights.at[p, rank],
+            send_sem=w_send.at[p, way, source_z], recv_sem=w_recv.at[p, rank],
+            device_id=where, device_id_type=MESH,
+        )
+
+    def hidden_copy(kind, c, source, where):
+        part = rows_all.at[c, pl.ds(source * tokens, tokens)]
+        return pltpu.make_async_remote_copy(
+            src_ref=part, dst_ref=part, send_sem=h_send.at[kind, c], recv_sem=h_recv.at[kind, c],
+            device_id={"uly": where}, device_id_type=MESH,
+        )
+
+    def kv_copy(source_z):
+        return pltpu.make_async_remote_copy(
+            src_ref=kv.at[source_z], dst_ref=kv.at[source_z],
+            send_sem=kv_send.at[source_z], recv_sem=kv_recv.at[source_z],
+            device_id=up, device_id_type=MESH,
+        )
+
+    def own_weights(p, finish=False):
+        act = (lambda c: c.wait_send()) if finish else (lambda c: c.start())
+
+        @pl.when(z < last)
+        def _():
+            act(weight_copy(p, 0, z, up, mine))
+
+        @pl.when(z > 0)
+        def _():
+            act(weight_copy(p, 1, z, down, mine))
+
+        act(weight_copy(p, 2, z, across, mine))
+
+    def pass_on(p, d, finish=False):
+        act = (lambda c: c.wait_send()) if finish else (lambda c: c.start())
+
+        @pl.when(z >= d)
+        def _():
+            rank = y * blk_n + z - d
+            if not finish:
+                weight_copy(p, 0, z - d, across, rank).wait_recv()
+
+            @pl.when(z < last)
+            def _():
+                act(weight_copy(p, 0, z - d, up, rank))
+
+            act(weight_copy(p, 2, z - d, across, rank))
+
+        @pl.when(z + d <= last)
+        def _():
+            rank = y * blk_n + z + d
+            if not finish:
+                weight_copy(p, 1, z + d, across, rank).wait_recv()
+
+            @pl.when(z > 0)
+            def _():
+                act(weight_copy(p, 1, z + d, down, rank))
+
+            act(weight_copy(p, 2, z + d, across, rank))
+
+    def across_arrived(p, d):
+        other = (1 - y) * blk_n
+        if d == 0:
+            weight_copy(p, 2, z, across, other + z).wait_recv()
+            return
+
+        @pl.when(z >= d)
+        def _():
+            weight_copy(p, 2, z - d, across, other + z - d).wait_recv()
+
+        @pl.when(z + d <= last)
+        def _():
+            weight_copy(p, 2, z + d, across, other + z + d).wait_recv()
+
+    def multiply(ps, c):
+        @pl.loop(0, group // PIECE)
+        def _(i):
+            at = pl.ds(pl.multiple_of(i * PIECE, PIECE), PIECE)
+            left = rows_all[c, at, :]
+            for p in ps:
+                acc[p, at, :] += jnp.dot(left, weights[p, c], preferred_element_type=jnp.float32)
+
+    def hidden_ready(c):
+        hidden_copy(0, c, core, core).wait_recv()
+        hidden_copy(2, c, far, core).wait_recv()
+
+    def turn(values, at):
+        return values * cos_ref[at, :] + pltpu.roll(values, HD // 2, 1) * sin_ref[at, :]
+
+    def query_chunks(d):
+        for p in range(1, pieces):
+            across_arrived(p, d)
+        ps = tuple(range(1, pieces))
+        if d == 0:
+            multiply(ps, mine)
+            multiply(ps, (1 - y) * blk_n + z)
+            return
+
+        @pl.when(z >= d)
+        def _():
+            multiply(ps, y * blk_n + z - d)
+            multiply(ps, (1 - y) * blk_n + z - d)
+
+        @pl.when(z + d <= last)
+        def _():
+            multiply(ps, y * blk_n + z + d)
+            multiply(ps, (1 - y) * blk_n + z + d)
+
+    def kv_pass(d):
+        @pl.when(z >= d)
+        def _():
+            kv_copy(z - d).wait_recv()
+
+            @pl.when(z < last)
+            def _():
+                kv_copy(z - d).start()
+
+    own[0].wait()
+    own[1].wait()
+    own_weights(0)
+    for c in range(chunks):
+        own[pieces + 1 + c].wait()
+        if c < 3:
+            hidden_copy(1, c, u, chip).start()
+    for c in range(chunks):
+        hidden_copy(0, c, u, core).start()
+    for p in range(1, pieces):
+        own[p + 1].wait()
+    acc[...] = jnp.zeros_like(acc)
+
+    chunk_ends = [-(-chunks * (s + 1) // HIDDEN_STEPS) for s in range(HIDDEN_STEPS)]
+    had = 0
+    multiplied = 0
+    step = 0
+    for p in range(pieces):
+        for d in range(1, blk_n):
+            if d == min(2, last) and p + 1 < pieces:
+                own_weights(p + 1)
+            pass_on(p, d)
+            if step < HIDDEN_STEPS:
+                for c in range(had, chunk_ends[step]):
+                    hidden_copy(1, c, chip, chip).wait_recv()
+                    hidden_copy(2, c, chip, core).start()
+                    if c + 3 < chunks:
+                        hidden_copy(1, c + 3, u, chip).start()
+                if p > 0:
+                    if multiplied == 0:
+                        for e in range(blk_n):
+                            across_arrived(0, e)
+                    for c in range(multiplied, had):
+                        hidden_ready(c)
+                        multiply((0,), c)
+                    multiplied = had
+                had = chunk_ends[step]
+            if p == pieces - 1:
+                query_chunks(d)
+                if d > 1:
+                    kv_pass(d - 1)
+            step += 1
+            if step == HIDDEN_STEPS:
+                for c in range(multiplied, chunks):
+                    hidden_ready(c)
+                    multiply((0,), c)
+
+                @pl.loop(0, group // PIECE)
+                def _(i):
+                    at = pl.ds(pl.multiple_of(i * PIECE, PIECE), PIECE)
+                    kv[z, at, :HD] = turn(acc[0, at, :HD], at).astype(jnp.bfloat16)
+                    kv[z, at, HD:] = acc[0, at, HD:].astype(jnp.bfloat16)
+
+                @pl.when(z < last)
+                def _():
+                    kv_copy(z).start()
+
+                query_chunks(0)
+
+    @pl.loop(0, group // PIECE)
+    def _(i):
+        at = pl.ds(pl.multiple_of(i * PIECE, PIECE), PIECE)
+        for p in range(1, pieces):
+            for half in range(PIECE // HD):
+                turned = turn(acc[p, at, half * HD : (half + 1) * HD], at)
+                col = (p - 1) * PIECE + half * HD
+                q_out[at, col : col + HD] = turned.astype(jnp.bfloat16)
+
+    kv_pass(last)
+
+    for e in range(blk_n):
+        @pl.when(e <= z)
+        def _(e=e):
+            pltpu.make_async_copy(kv.at[e], kv_out.at[pl.ds(e * group, group)], local_sem.at[e]).start()
+
+    for p in range(pieces):
+        own_weights(p, finish=True)
+        for d in range(1, blk_n):
+            pass_on(p, d, finish=True)
+    for c in range(chunks):
+        hidden_copy(0, c, u, core).wait_send()
+        hidden_copy(1, c, u, chip).wait_send()
+        hidden_copy(2, c, chip, core).wait_send()
+    for e in range(blk_n):
+        @pl.when(e <= z)
+        def _(e=e):
+            @pl.when(z < last)
+            def _():
+                kv_copy(e).wait_send()
+
+            pltpu.make_async_copy(kv.at[e], kv_out.at[pl.ds(e * group, group)], local_sem.at[e]).wait()
+
+
+def project(hid, wq, wk, wv, cosine, sine, dp_n, blk_n, uly_n):
+    tokens, width = hid.shape
+    depth, query_cols = wq.shape
+    chunks = dp_n * blk_n
+    group = tokens * uly_n
+    pieces = 1 + query_cols // PIECE
+    hbm = pl.BlockSpec(memory_space=pl.ANY)
+    vmem = pl.BlockSpec(memory_space=pltpu.VMEM)
+    return pl.pallas_call(
+        functools.partial(project_kernel, dp_n, blk_n),
+        out_shape=(
+            jax.ShapeDtypeStruct((group, query_cols), jnp.bfloat16),
+            jax.ShapeDtypeStruct((blk_n * group, 2 * HD), jnp.bfloat16),
+        ),
+        in_specs=[hbm, hbm, hbm, hbm, vmem, vmem],
+        out_specs=(vmem, hbm),
+        scratch_shapes=[
+            pltpu.VMEM((pieces, chunks, depth, PIECE), jnp.bfloat16),
+            pltpu.VMEM((chunks, group, depth), jnp.bfloat16),
+            pltpu.VMEM((pieces, group, PIECE), jnp.float32),
+            pltpu.VMEM((blk_n, group, 2 * HD), jnp.bfloat16),
+            pltpu.SemaphoreType.DMA((pieces + 1 + chunks,)),
+            pltpu.SemaphoreType.DMA((pieces, 3, blk_n)),
+            pltpu.SemaphoreType.DMA((pieces, chunks)),
+            pltpu.SemaphoreType.DMA((3, chunks)),
+            pltpu.SemaphoreType.DMA((3, chunks)),
+            pltpu.SemaphoreType.DMA((blk_n,)),
+            pltpu.SemaphoreType.DMA((blk_n,)),
+        ],
+        compiler_params=pltpu.CompilerParams(
+            collective_id=0, has_side_effects=True, vmem_limit_bytes=50 * 1024 * 1024
+        ),
+        cost_estimate=pl.CostEstimate(
+            flops=2 * group * width * (query_cols + 2 * HD), bytes_accessed=8 * 10**6, transcendentals=0
+        ),
+    )(hid, wq, wk, wv, cosine, sine)
+
+
 def shards(hidden_states, block_table, w_query, w_key, w_value):
     tokens = hidden_states.shape[1]
     uly_size = lax.axis_size("uly")
@@ -116,6 +423,25 @@
     query_cols = heads_here * HD
     group_rows = tokens * uly_size
     tiles = group_rows // MBLK
+    dp_n, blk_n = lax.axis_size("dp"), lax.axis_size("blk")
+    if dp_n == 2 and blk_n == 4 and uly_size == 4 and repeats == 1 and query_cols % PIECE == 0:
+        positions = blk_rank * group_rows + jnp.arange(group_rows, dtype=jnp.int32)
+        cosine, sine = angle_tables(positions)
+        query, key_value = project(
+            hidden_states[0],
+            w_query,
+            w_key,
+            w_value,
+            jnp.concatenate([cosine, cosine], axis=1),
+            jnp.concatenate([-sine, sine], axis=1),
+            dp_n,
+            blk_n,
+            uly_size,
+        )
+        result = attend(
+            block_table[0], blk_rank[None].astype(jnp.int32), query, key_value, heads_here, tiles
+        )
+        return lax.all_to_all(result, "uly", split_axis=0, concat_axis=1, tiled=True)[None]
     w_joined = jnp.concatenate([w_query, w_key, w_value], axis=1)
     w_rows = lax.all_gather(w_joined, ("dp", "blk"), axis=0, tiled=True)
     projected = jnp.dot(

time: 277 us -> 153 us (0.55)
  waiting for transfers between devices: 193 us -> 0 us
  Pallas kernels: 22.7 us -> 128 us
  between operations: 13.2 us -> 0.11 us
  matrix products: 10.9 us -> 0 us
  other arithmetic: 11.6 us -> 2.25 us
  local copies, waits for them, and re-layouts: 7.92 us -> 4.01 us
    all_gather x3 -> x0, waiting for transfers between devices: 192 us -> none  [the longest x1 97.1 us: shards(): w_rows = lax.all_gather(w_joined, ('dp', 'blk'), axis=0, tiled=True)]
    pallas_call x0 -> x1, Pallas kernels: none -> 108 us  [project(): pl.pallas_call(functools.partial(project_kernel, dp_n, blk_n), out_shape=...]
    dot_general x1 -> x0, matrix products: 10.9 us -> none  [shards(): jnp.dot(lax.all_gather(hidden_states[0], 'uly', axis=0, tiled=True), w_ro...]
    concatenate x3 -> x1, other arithmetic: 4.4 us -> 0.34 us  [shards(): jnp.concatenate([cosine, cosine], axis=1)]
    another operation x2 -> x0, other arithmetic: 4.03 us -> none
    cos x1 -> x0, other arithmetic: 3.05 us -> none  [angle_tables(): return (jnp.cos(angles), jnp.sin(angles))]
  transfers between devices with their start and end apart: 3 -> 0, of which waited for: 3 -> 0; matrix products, arithmetic and copies ran while one was open for 4% -> 0% of each run, Pallas kernels for 0% -> 0%
where the time goes in v1:
time: 153 us; the launch traced here: 151 us
  Pallas kernels  128 us (84%)
  blocking collectives  16.9 us (11%)
  local copies, waits for them, and re-layouts  4.01 us (3%)
  other arithmetic  2.25 us (1%)
    pallas_call x1, Pallas kernels, project(): pl.pallas_call(functools.partial(project_kernel, dp_n, blk_n), out_shape=...  108 us
    pallas_call x1, Pallas kernels, attend(): pl.pallas_call(functools.partial(attend_kernel, heads, tiles), out_shape=...  20.4 us
    all_to_all x1, blocking collectives, shards(): lax.all_to_all(result, 'uly', split_axis=0, concat_axis=1, tiled=True)[None]  16.9 us

profile of v1, /device:TPU:28, one launch (start us, length us, event | category | flops | bytes accessed | tf_op | source)
XLA Modules:
  0.0 151.4 jit_solution(1734260340590009771)
XLA Ops:
  0.0 0.0 copy-start
  0.0 0.0 copy-start.1
  0.1 0.0 copy-start.2
  0.1 1.9 %fusion = (f32[1024,64]{1,0:T(8,128)S(1)}, f32[1024,64]{1,0:T(8,128)S(1)}, f32[1024,64]{1,0:T(8,128)S(1)}) fusion(f32[64]{0:T(128)S(1)} %negate_power_fusion, f32[1024]{0:T(1024)S(1)} %add_convert_fusion), kind=kLoop, calls=%fused_computation.4 | loop fusion | flops 131072 | bytes 790784 | tf_op jit(solution)/shard_map/neg | solution.py:436
  2.0 0.3 pad_maximum_fusion
  2.3 0.0 copy-done
  2.3 0.0 copy-done.1
  2.3 0.0 copy-done.2
  2.3 0.0 copy-start.3
  2.4 107.7 %shard_map.55 = (bf16[1024,512]{1,0:T(8,128)(2,1)S(1)}, bf16[4096,256]{1,0:T(8,128)(2,1)}) custom-call(bf16[256,4096]{1,0:T(8,128)(2,1)} %bitcast.8, bf16[512,512]{1,0:T(8,128)(2,1)S(1)} %copy-done, bf16[512,128]{1,0:T(8,128)(2,1)S(1)} %copy-done.1, bf16[512,128]{1,0:T(8,128)(2,1)S(1)} %copy-done.2, f32[1024,128]{1,0:T(8,128)S(1)} %get-tuple-element.12.cos_ref, ...), custom_call_target="tpu_custom_call" | custom-call | flops 6442450944 | bytes 8000000 | tf_op jit(solution)/shard_map/pallas_call | solution.py:385
  110.1 0.0 copy-done.3
  110.1 0.0 copy-start.4
  110.1 1.6 %copy-done.4 = bf16[4096,256]{1,0:T(8,128)(2,1)S(1)} copy-done((bf16[4096,256]{1,0:T(8,128)(2,1)S(1)}, bf16[4096,256]{1,0:T(8,128)(2,1)}, u32[]{:S(2)}) %copy-start.4) | copy-done | bytes 2097176
  111.7 20.4 %shard_map.56 = bf16[1024,512]{1,0:T(8,128)(2,1)S(1)} custom-call(s32[8,8]{1,0:T(8,128)S(1)} %bitcast.6, s32[1]{0:T(128)} %bitcast.1.rank, bf16[1024,512]{1,0:T(8,128)(2,1)S(1)} %get-tuple-element.7.q_ref, bf16[4096,256]{1,0:T(8,128)(2,1)S(1)} %copy-done.4), custom_call_target="tpu_custom_call" | custom-call | flops 8000000000 | bytes 4000000 | tf_op jit(solution)/shard_map/pallas_call | solution.py:93
  132.1 16.9 %all_to_all.16 = bf16[4,256,512]{2,1,0:T(8,128)(2,1)S(1)} all-to-all(bf16[4,256,512]{2,1,0:T(8,128)(2,1)S(1)} %bitcast.5), channel_id=1, replica_groups=mesh['dp'=2,'blk'=4,'uly'=4] {'uly'}, dimensions={0} | all-to-all | bytes 2097152 | tf_op jit(solution)/shard_map/all_to_all | solution.py:444
  149.0 0.8 copy.6
  149.8 1.6 %broadcast_in_dim.9 = bf16[1,256,2048]{2,1,0:T(8,128)(2,1)} reshape(bf16[256,4,512]{2,1,0:T(4,128)(2,1)S(1)} %copy.6) | data formatting | bytes 2097152 | tf_op jit(solution)/shard_map/broadcast_in_dim | solution.py:444
  (2 shorter events, 0.0 us)
Async XLA Ops:
  0.0 2.3 %copy-start = (bf16[512,512]{1,0:T(8,128)(2,1)S(1)}, bf16[512,512]{1,0:T(8,128)(2,1)}, u32[]{:S(2)}) copy-start(bf16[512,512]{1,0:T(8,128)(2,1)} %wq.1) | copy-start | bytes 1572868
  0.0 2.3 %copy-start.1 = (bf16[512,128]{1,0:T(8,128)(2,1)S(1)}, bf16[512,128]{1,0:T(8,128)(2,1)}, u32[]{:S(2)}) copy-start(bf16[512,128]{1,0:T(8,128)(2,1)} %wk.1) | copy-start | bytes 393220
  0.1 2.3 %copy-start.2 = (bf16[512,128]{1,0:T(8,128)(2,1)S(1)}, bf16[512,128]{1,0:T(8,128)(2,1)}, u32[]{:S(2)}) copy-start(bf16[512,128]{1,0:T(8,128)(2,1)} %wv.1) | copy-start | bytes 393220
  2.3 107.7 %copy-start.3 = (s32[1,8,8]{2,1,0:T(8,128)S(1)}, s32[1,8,8]{2,1,0:T(8,128)}, u32[]{:S(2)}) copy-start(s32[1,8,8]{2,1,0:T(8,128)} %param.6) | copy-start | bytes 772
  110.1 1.6 %copy-start.4 = (bf16[4096,256]{1,0:T(8,128)(2,1)S(1)}, bf16[4096,256]{1,0:T(8,128)(2,1)}, u32[]{:S(2)}) copy-start(bf16[4096,256]{1,0:T(8,128)(2,1)} %get-tuple-element.8.kv_ref) | copy-start | bytes 6291460

commit v2 on v1

--- a/solution.py
+++ b/solution.py
@@ -110,9 +110,10 @@
 HIDDEN_STEPS = 6
 
 
-def project_kernel(
-    dp_n, blk_n, hid, wq, wk, wv, cos_ref, sin_ref, q_out, kv_out,
-    weights, rows_all, acc, kv, local_sem, w_send, w_recv, h_send, h_recv, kv_send, kv_recv,
+def fused_kernel(
+    dp_n, blk_n, table, hid, wq, wk, wv, cos_ref, sin_ref, out,
+    weights, rows_all, acc, kv, q_rows, done, best, total, accum,
+    local_sem, w_send, w_recv, h_send, h_recv, kv_send, kv_recv, o_send, o_recv,
 ):
     y, z, u = lax.axis_index("dp"), lax.axis_index("blk"), lax.axis_index("uly")
     last = blk_n - 1
@@ -137,7 +138,7 @@
     def _():
         pl.semaphore_signal(barrier, inc=1, device_id=down, device_id_type=MESH)
 
-    for where in (across, {"uly": core}, {"uly": chip}):
+    for where in (across, {"uly": core}, {"uly": chip}, {"uly": far}):
         pl.semaphore_signal(barrier, inc=1, device_id=where, device_id_type=MESH)
 
     own = [
@@ -161,7 +162,7 @@
     for copy in own:
         copy.start()
     middle = jnp.where((z > 0) & (z < last), 1, 0)
-    pl.semaphore_wait(barrier, 4 + middle)
+    pl.semaphore_wait(barrier, 5 + middle)
 
     def weight_copy(p, way, source_z, where, rank):
         return pltpu.make_async_remote_copy(
@@ -300,7 +301,7 @@
     step = 0
     for p in range(pieces):
         for d in range(1, blk_n):
-            if d == min(2, last) and p + 1 < pieces:
+            if d == 1 and p + 1 < pieces:
                 own_weights(p + 1)
             pass_on(p, d)
             if step < HIDDEN_STEPS:
@@ -347,14 +348,114 @@
             for half in range(PIECE // HD):
                 turned = turn(acc[p, at, half * HD : (half + 1) * HD], at)
                 col = (p - 1) * PIECE + half * HD
-                q_out[at, col : col + HD] = turned.astype(jnp.bfloat16)
-
-    kv_pass(last)
-
-    for e in range(blk_n):
-        @pl.when(e <= z)
-        def _(e=e):
-            pltpu.make_async_copy(kv.at[e], kv_out.at[pl.ds(e * group, group)], local_sem.at[e]).start()
+                q_rows[at, col : col + HD] = turned.astype(jnp.bfloat16)
+
+    scale = HD**-0.5 * LOG2E
+    tiles = group // MBLK
+    heads = q_rows.shape[1] // HD
+    query_cols = q_rows.shape[1]
+
+    def visit(q_tile, source_z, k_tile, first):
+        keys = kv.at[source_z, pl.ds(pl.multiple_of(k_tile * MBLK, MBLK), MBLK)]
+        key, value = keys[:, :HD], keys[:, HD:]
+        q_at = pl.ds(pl.multiple_of(q_tile * MBLK, MBLK), MBLK)
+        allowed = table[z * tiles + q_tile, source_z * tiles + k_tile]
+        bias = jnp.where(allowed > 0, 0.0, -1e30).astype(jnp.float32)
+        for head in range(heads):
+            cols = slice(head * MBLK, (head + 1) * MBLK)
+            query = q_rows[q_at, head * HD : (head + 1) * HD]
+            scores = lax.dot_general(key, query, NT, preferred_element_type=jnp.float32) * scale
+            if first:
+                key_at = lax.broadcasted_iota(jnp.int32, (MBLK, MBLK), 0)
+                query_at = lax.broadcasted_iota(jnp.int32, (MBLK, MBLK), 1)
+                scores = jnp.where(key_at <= query_at, scores, -1e30)
+                new_best = jnp.max(scores, axis=0, keepdims=True)
+            else:
+                scores = scores + bias
+                old_best = best[q_tile, :, cols]
+                new_best = jnp.maximum(old_best, jnp.max(scores, axis=0, keepdims=True))
+            grown = jnp.exp2(scores - new_best)
+            sums = jnp.sum(grown, axis=0, keepdims=True)
+            mixed = lax.dot_general(
+                value, grown.astype(jnp.bfloat16), TN, preferred_element_type=jnp.float32
+            )
+            best[q_tile, :, cols] = new_best
+            if first:
+                total[q_tile, :, cols] = sums
+                accum[q_tile, :, cols] = mixed
+            else:
+                rescale = jnp.exp2(old_best - new_best)
+                total[q_tile, :, cols] = total[q_tile, :, cols] * rescale + sums
+                accum[q_tile, :, cols] = accum[q_tile, :, cols] * rescale + mixed
+
+    def out_copy(owner):
+        return pltpu.make_async_remote_copy(
+            src_ref=done.at[pl.ds(owner * tokens, tokens)],
+            dst_ref=out.at[:, pl.ds(pl.multiple_of(u * query_cols, query_cols), query_cols)],
+            send_sem=o_send.at[owner], recv_sem=o_recv.at[u],
+            device_id={"uly": owner}, device_id_type=MESH,
+        )
+
+    def out_arrival(source):
+        return pltpu.make_async_remote_copy(
+            src_ref=done.at[pl.ds(source * tokens, tokens)],
+            dst_ref=out.at[:, pl.ds(pl.multiple_of(source * query_cols, query_cols), query_cols)],
+            send_sem=o_send.at[source], recv_sem=o_recv.at[source],
+            device_id={"uly": source}, device_id_type=MESH,
+        )
+
+    def out_own():
+        return pltpu.make_async_copy(
+            done.at[pl.ds(u * tokens, tokens)],
+            out.at[:, pl.ds(pl.multiple_of(u * query_cols, query_cols), query_cols)],
+            local_sem.at[0],
+        )
+
+    def finalize(q_tile):
+        q_at = pl.ds(pl.multiple_of(q_tile * MBLK, MBLK), MBLK)
+        for head in range(heads):
+            cols = slice(head * MBLK, (head + 1) * MBLK)
+            final = accum[q_tile, :, cols] / total[q_tile, :, cols]
+            done[q_at, head * HD : (head + 1) * HD] = final.T.astype(jnp.bfloat16)
+        owners = MBLK // tokens
+        for e in range(owners):
+            owner = q_tile * owners + e
+
+            @pl.when(owner != u)
+            def _():
+                out_copy(owner).start()
+
+            @pl.when(owner == u)
+            def _():
+                out_own().start()
+
+    @pl.loop(0, tiles)
+    def _(q_tile):
+        visit(q_tile, z, q_tile, True)
+
+        @pl.loop(0, q_tile)
+        def _(k_tile):
+            visit(q_tile, z, k_tile, False)
+
+        @pl.when(z == 0)
+        def _():
+            finalize(q_tile)
+
+    for d in range(1, blk_n):
+        if d == last:
+            kv_pass(d)
+
+        @pl.when(z >= d)
+        def _(d=d):
+            @pl.loop(0, tiles)
+            def _(q_tile):
+                @pl.loop(0, tiles)
+                def _(k_tile):
+                    visit(q_tile, z - d, k_tile, False)
+
+                @pl.when(z == d)
+                def _():
+                    finalize(q_tile)
 
     for p in range(pieces):
         own_weights(p, finish=True)
@@ -371,30 +472,36 @@
             def _():
                 kv_copy(e).wait_send()
 
-            pltpu.make_async_copy(kv.at[e], kv_out.at[pl.ds(e * group, group)], local_sem.at[e]).wait()
-
-
-def project(hid, wq, wk, wv, cosine, sine, dp_n, blk_n, uly_n):
+    out_own().wait()
+    for other in (core, chip, far):
+        out_copy(other).wait_send()
+        out_arrival(other).wait_recv()
+
+
+def fused(table, hid, wq, wk, wv, cosine, sine, dp_n, blk_n, uly_n):
     tokens, width = hid.shape
     depth, query_cols = wq.shape
     chunks = dp_n * blk_n
     group = tokens * uly_n
     pieces = 1 + query_cols // PIECE
+    tiles, heads = group // MBLK, query_cols // HD
     hbm = pl.BlockSpec(memory_space=pl.ANY)
     vmem = pl.BlockSpec(memory_space=pltpu.VMEM)
     return pl.pallas_call(
-        functools.partial(project_kernel, dp_n, blk_n),
-        out_shape=(
-            jax.ShapeDtypeStruct((group, query_cols), jnp.bfloat16),
-            jax.ShapeDtypeStruct((blk_n * group, 2 * HD), jnp.bfloat16),
-        ),
-        in_specs=[hbm, hbm, hbm, hbm, vmem, vmem],
-        out_specs=(vmem, hbm),
+        functools.partial(fused_kernel, dp_n, blk_n),
+        out_shape=jax.ShapeDtypeStruct((tokens, uly_n * query_cols), jnp.bfloat16),
+        in_specs=[pl.BlockSpec(memory_space=pltpu.SMEM), hbm, hbm, hbm, hbm, vmem, vmem],
+        out_specs=hbm,
         scratch_shapes=[
             pltpu.VMEM((pieces, chunks, depth, PIECE), jnp.bfloat16),
             pltpu.VMEM((chunks, group, depth), jnp.bfloat16),
             pltpu.VMEM((pieces, group, PIECE), jnp.float32),
             pltpu.VMEM((blk_n, group, 2 * HD), jnp.bfloat16),
+            pltpu.VMEM((group, query_cols), jnp.bfloat16),
+            pltpu.VMEM((group, query_cols), jnp.bfloat16),
+            pltpu.VMEM((tiles, 1, heads * MBLK), jnp.float32),
+            pltpu.VMEM((tiles, 1, heads * MBLK), jnp.float32),
+            pltpu.VMEM((tiles, HD, heads * MBLK), jnp.float32),
             pltpu.SemaphoreType.DMA((pieces + 1 + chunks,)),
             pltpu.SemaphoreType.DMA((pieces, 3, blk_n)),
             pltpu.SemaphoreType.DMA((pieces, chunks)),
@@ -402,6 +509,8 @@
             pltpu.SemaphoreType.DMA((3, chunks)),
             pltpu.SemaphoreType.DMA((blk_n,)),
             pltpu.SemaphoreType.DMA((blk_n,)),
+            pltpu.SemaphoreType.DMA((uly_n,)),
+            pltpu.SemaphoreType.DMA((uly_n,)),
         ],
         compiler_params=pltpu.CompilerParams(
             collective_id=0, has_side_effects=True, vmem_limit_bytes=50 * 1024 * 1024
@@ -409,7 +518,7 @@
         cost_estimate=pl.CostEstimate(
             flops=2 * group * width * (query_cols + 2 * HD), bytes_accessed=8 * 10**6, transcendentals=0
         ),
-    )(hid, wq, wk, wv, cosine, sine)
+    )(table, hid, wq, wk, wv, cosine, sine)
 
 
 def shards(hidden_states, block_table, w_query, w_key, w_value):
@@ -427,7 +536,8 @@
     if dp_n == 2 and blk_n == 4 and uly_size == 4 and repeats == 1 and query_cols % PIECE == 0:
         positions = blk_rank * group_rows + jnp.arange(group_rows, dtype=jnp.int32)
         cosine, sine = angle_tables(positions)
-        query, key_value = project(
+        merged = fused(
+            block_table[0],
             hidden_states[0],
             w_query,
             w_key,
@@ -438,10 +548,7 @@
             blk_n,
             uly_size,
         )
-        result = attend(
-            block_table[0], blk_rank[None].astype(jnp.int32), query, key_value, heads_here, tiles
-        )
-        return lax.all_to_all(result, "uly", split_axis=0, concat_axis=1, tiled=True)[None]
+        return merged[None]
     w_joined = jnp.concatenate([w_query, w_key, w_value], axis=1)
     w_rows = lax.all_gather(w_joined, ("dp", "blk"), axis=0, tiled=True)
     projected = jnp.dot(

time: 153 us -> 143 us (0.935)
  blocking collectives: 16.9 us -> 0 us
  Pallas kernels: 128 us -> 139 us
  local copies, waits for them, and re-layouts: 4.01 us -> 1 us
    all_to_all x1 -> x0, blocking collectives: 16.9 us -> none  [shards(): lax.all_to_all(result, 'uly', split_axis=0, concat_axis=1, tiled=True)[None]]
    pallas_call x2 -> x1, Pallas kernels: 128 us -> 139 us  [fused(): pl.pallas_call(functools.partial(fused_kernel, dp_n, blk_n), out_shape=ja...]
    broadcast_in_dim x1 -> x0, local copies, waits for them, and re-layouts: 1.59 us -> none  [shards(): lax.all_to_all(result, 'uly', split_axis=0, concat_axis=1, tiled=True)[None]]
where the time goes in v2:
time: 143 us; the launch traced here: 142 us
  Pallas kernels  139 us (97%)
  other arithmetic  2.25 us (2%)
    pallas_call x1, Pallas kernels, fused(): pl.pallas_call(functools.partial(fused_kernel, dp_n, blk_n), out_shape=ja...  139 us

profile of v2, /device:TPU:28, one launch (start us, length us, event | category | flops | bytes accessed | tf_op | source)
XLA Modules:
  0.0 141.9 jit_solution(17721375854261616172)
XLA Ops:
  0.0 0.0 copy-start
  0.0 0.0 copy-start.1
  0.0 0.0 copy-start.2
  0.1 0.0 copy-start.3
  0.1 1.9 %fusion = (f32[1024,64]{1,0:T(8,128)S(1)}, f32[1024,64]{1,0:T(8,128)S(1)}, f32[1024,64]{1,0:T(8,128)S(1)}) fusion(f32[64]{0:T(128)S(1)} %negate_power_fusion, f32[1024]{0:T(1024)S(1)} %add_convert_fusion), kind=kLoop, calls=%fused_computation.4 | loop fusion | flops 131072 | bytes 790784 | tf_op jit(solution)/shard_map/neg | solution.py:546
  2.0 0.3 pad_maximum_fusion
  2.3 0.0 copy-done
  2.3 0.0 copy-done.1
  2.3 0.0 copy-done.2
  2.4 0.0 copy-done.3
  2.4 138.6 %shard_map.55 = bf16[256,2048]{1,0:T(8,128)(2,1)S(1)} custom-call(s32[8,8]{1,0:T(8,128)S(1)} %bitcast.4, bf16[256,4096]{1,0:T(8,128)(2,1)} %bitcast.5, bf16[512,512]{1,0:T(8,128)(2,1)S(1)} %copy-done, bf16[512,128]{1,0:T(8,128)(2,1)S(1)} %copy-done.1, bf16[512,128]{1,0:T(8,128)(2,1)S(1)} %copy-done.2, f32[1024,128]{1,0:T(8,128)S(1)} %get-tuple-element.8.cos_ref, ...), custom_call_target="tpu_custom_call" | custom-call | flops 6442450944 | bytes 8000000 | tf_op jit(solution)/shard_map/pallas_call | solution.py:490
  141.0 1.0 copy.7
  (2 shorter events, 0.0 us)
Async XLA Ops:
  0.0 2.3 %copy-start = (bf16[512,512]{1,0:T(8,128)(2,1)S(1)}, bf16[512,512]{1,0:T(8,128)(2,1)}, u32[]{:S(2)}) copy-start(bf16[512,512]{1,0:T(8,128)(2,1)} %wq.1) | copy-start | bytes 1572868
  0.0 2.3 %copy-start.1 = (bf16[512,128]{1,0:T(8,128)(2,1)S(1)}, bf16[512,128]{1,0:T(8,128)(2,1)}, u32[]{:S(2)}) copy-start(bf16[512,128]{1,0:T(8,128)(2,1)} %wk.1) | copy-start | bytes 393220
  0.0 2.3 %copy-start.2 = (bf16[512,128]{1,0:T(8,128)(2,1)S(1)}, bf16[512,128]{1,0:T(8,128)(2,1)}, u32[]{:S(2)}) copy-start(bf16[512,128]{1,0:T(8,128)(2,1)} %wv.1) | copy-start | bytes 393220
  0.1 2.3 %copy-start.3 = (s32[1,8,8]{2,1,0:T(8,128)S(1)}, s32[1,8,8]{2,1,0:T(8,128)}, u32[]{:S(2)}) copy-start(s32[1,8,8]{2,1,0:T(8,128)} %param.6) | copy-start | bytes 772

commit v3 on v2

--- a/solution.py
+++ b/solution.py
@@ -107,7 +107,7 @@
 
 PIECE = 256
 MESH = pl.DeviceIdType.MESH
-HIDDEN_STEPS = 6
+IN_FLIGHT = 4
 
 
 def fused_kernel(
@@ -178,10 +178,17 @@
             device_id={"uly": where}, device_id_type=MESH,
         )
 
-    def kv_copy(source_z):
+    own_tile = u // 2
+
+    def tile_rows(half):
+        tile = own_tile if half == 0 else 1 - own_tile
+        return pl.multiple_of(tile * MBLK, MBLK)
+
+    def kv_copy(source_z, half):
+        part = kv.at[source_z, pl.ds(tile_rows(half), MBLK)]
         return pltpu.make_async_remote_copy(
-            src_ref=kv.at[source_z], dst_ref=kv.at[source_z],
-            send_sem=kv_send.at[source_z], recv_sem=kv_recv.at[source_z],
+            src_ref=part, dst_ref=part,
+            send_sem=kv_send.at[half, source_z], recv_sem=kv_recv.at[half, source_z],
             device_id=up, device_id_type=MESH,
         )
 
@@ -239,55 +246,87 @@
         def _():
             weight_copy(p, 2, z + d, across, other + z + d).wait_recv()
 
-    def multiply(ps, c):
+    def multiply(c):
         @pl.loop(0, group // PIECE)
         def _(i):
             at = pl.ds(pl.multiple_of(i * PIECE, PIECE), PIECE)
-            left = rows_all[c, at, :]
-            for p in ps:
-                acc[p, at, :] += jnp.dot(left, weights[p, c], preferred_element_type=jnp.float32)
-
-    def hidden_ready(c):
-        hidden_copy(0, c, core, core).wait_recv()
-        hidden_copy(2, c, far, core).wait_recv()
+            acc[at, :] += jnp.dot(
+                rows_all[c, at, :], weights[pieces - 1, c], preferred_element_type=jnp.float32
+            )
+
+    def whole_sum(p, at):
+        result = jnp.dot(rows_all[0, at, :], weights[p, 0], preferred_element_type=jnp.float32)
+        for c in range(1, chunks):
+            result += jnp.dot(rows_all[c, at, :], weights[p, c], preferred_element_type=jnp.float32)
+        return result
 
     def turn(values, at):
         return values * cos_ref[at, :] + pltpu.roll(values, HD // 2, 1) * sin_ref[at, :]
 
+    def kv_half(half):
+        @pl.loop(0, MBLK // PIECE)
+        def _(i):
+            at = pl.ds(pl.multiple_of(tile_rows(half) + i * PIECE, PIECE), PIECE)
+            both = whole_sum(0, at)
+            kv[z, at, :HD] = turn(both[:, :HD], at).astype(jnp.bfloat16)
+            kv[z, at, HD:] = both[:, HD:].astype(jnp.bfloat16)
+
+        @pl.when(z < last)
+        def _():
+            kv_copy(z, half).start()
+
+    def keep_query(p, at, values):
+        for half in range(PIECE // HD):
+            col = (p - 1) * PIECE + half * HD
+            turned = turn(values[:, half * HD : (half + 1) * HD], at)
+            q_rows[at, col : col + HD] = turned.astype(jnp.bfloat16)
+
+    def whole_queries(lower, upper):
+        @pl.loop(lower, upper)
+        def _(i):
+            at = pl.ds(pl.multiple_of(i * PIECE, PIECE), PIECE)
+            for p in range(1, pieces - 1):
+                keep_query(p, at, whole_sum(p, at))
+
     def query_chunks(d):
-        for p in range(1, pieces):
-            across_arrived(p, d)
-        ps = tuple(range(1, pieces))
+        across_arrived(pieces - 1, d)
         if d == 0:
-            multiply(ps, mine)
-            multiply(ps, (1 - y) * blk_n + z)
+            multiply(mine)
+            multiply((1 - y) * blk_n + z)
             return
 
         @pl.when(z >= d)
         def _():
-            multiply(ps, y * blk_n + z - d)
-            multiply(ps, (1 - y) * blk_n + z - d)
+            multiply(y * blk_n + z - d)
+            multiply((1 - y) * blk_n + z - d)
 
         @pl.when(z + d <= last)
         def _():
-            multiply(ps, y * blk_n + z + d)
-            multiply(ps, (1 - y) * blk_n + z + d)
-
-    def kv_pass(d):
+            multiply(y * blk_n + z + d)
+            multiply((1 - y) * blk_n + z + d)
+
+    def kv_pass(d, half):
         @pl.when(z >= d)
         def _():
-            kv_copy(z - d).wait_recv()
+            kv_copy(z - d, half).wait_recv()
 
             @pl.when(z < last)
             def _():
-                kv_copy(z - d).start()
+                kv_copy(z - d, half).start()
+
+    def hidden_step(lower, upper):
+        for c in range(lower, upper):
+            hidden_copy(1, c, chip, chip).wait_recv()
+            hidden_copy(2, c, chip, core).start()
+            if c + IN_FLIGHT < chunks:
+                hidden_copy(1, c + IN_FLIGHT, u, chip).start()
 
     own[0].wait()
     own[1].wait()
     own_weights(0)
     for c in range(chunks):
         own[pieces + 1 + c].wait()
-        if c < 3:
+        if c < IN_FLIGHT:
             hidden_copy(1, c, u, chip).start()
     for c in range(chunks):
         hidden_copy(0, c, u, core).start()
@@ -295,60 +334,47 @@
         own[p + 1].wait()
     acc[...] = jnp.zeros_like(acc)
 
-    chunk_ends = [-(-chunks * (s + 1) // HIDDEN_STEPS) for s in range(HIDDEN_STEPS)]
-    had = 0
-    multiplied = 0
+    slabs = group // PIECE
+    ends = (0, 1, 3, 5, 7, 8)
     step = 0
     for p in range(pieces):
         for d in range(1, blk_n):
             if d == 1 and p + 1 < pieces:
                 own_weights(p + 1)
             pass_on(p, d)
-            if step < HIDDEN_STEPS:
-                for c in range(had, chunk_ends[step]):
-                    hidden_copy(1, c, chip, chip).wait_recv()
-                    hidden_copy(2, c, chip, core).start()
-                    if c + 3 < chunks:
-                        hidden_copy(1, c + 3, u, chip).start()
-                if p > 0:
-                    if multiplied == 0:
-                        for e in range(blk_n):
-                            across_arrived(0, e)
-                    for c in range(multiplied, had):
-                        hidden_ready(c)
-                        multiply((0,), c)
-                    multiplied = had
-                had = chunk_ends[step]
-            if p == pieces - 1:
-                query_chunks(d)
-                if d > 1:
-                    kv_pass(d - 1)
+            if 0 < step < len(ends):
+                hidden_step(ends[step - 1], ends[step])
+            if step == 3:
+                for e in range(blk_n):
+                    across_arrived(0, e)
+                for c in range(chunks):
+                    hidden_copy(0, c, core, core).wait_recv()
+                kv_half(0)
+            elif step == 5:
+                kv_pass(1, 0)
+                for c in range(chunks):
+                    hidden_copy(2, c, far, core).wait_recv()
+                kv_half(1)
+            elif step == 6:
+                query_chunks(0)
+            elif step == 7:
+                kv_pass(2, 0)
+                kv_pass(1, 1)
+                for e in range(blk_n):
+                    across_arrived(1, e)
+                whole_queries(0, slabs // 2)
+                query_chunks(1)
+            elif step == 8:
+                whole_queries(slabs // 2, slabs)
+                query_chunks(2)
+                kv_pass(2, 1)
+                query_chunks(3)
             step += 1
-            if step == HIDDEN_STEPS:
-                for c in range(multiplied, chunks):
-                    hidden_ready(c)
-                    multiply((0,), c)
-
-                @pl.loop(0, group // PIECE)
-                def _(i):
-                    at = pl.ds(pl.multiple_of(i * PIECE, PIECE), PIECE)
-                    kv[z, at, :HD] = turn(acc[0, at, :HD], at).astype(jnp.bfloat16)
-                    kv[z, at, HD:] = acc[0, at, HD:].astype(jnp.bfloat16)
-
-                @pl.when(z < last)
-                def _():
-                    kv_copy(z).start()
-
-                query_chunks(0)
-
-    @pl.loop(0, group // PIECE)
+
+    @pl.loop(0, slabs)
     def _(i):
         at = pl.ds(pl.multiple_of(i * PIECE, PIECE), PIECE)
-        for p in range(1, pieces):
-            for half in range(PIECE // HD):
-                turned = turn(acc[p, at, half * HD : (half + 1) * HD], at)
-                col = (p - 1) * PIECE + half * HD
-                q_rows[at, col : col + HD] = turned.astype(jnp.bfloat16)
+        keep_query(pieces - 1, at, acc[at, :])
 
     scale = HD**-0.5 * LOG2E
     tiles = group // MBLK
@@ -443,7 +469,8 @@
 
     for d in range(1, blk_n):
         if d == last:
-            kv_pass(d)
+            kv_pass(d, 0)
+            kv_pass(d, 1)
 
         @pl.when(z >= d)
         def _(d=d):
@@ -470,7 +497,8 @@
         def _(e=e):
             @pl.when(z < last)
             def _():
-                kv_copy(e).wait_send()
+                kv_copy(e, 0).wait_send()
+                kv_copy(e, 1).wait_send()
 
     out_own().wait()
     for other in (core, chip, far):
@@ -495,7 +523,7 @@
         scratch_shapes=[
             pltpu.VMEM((pieces, chunks, depth, PIECE), jnp.bfloat16),
             pltpu.VMEM((chunks, group, depth), jnp.bfloat16),
-            pltpu.VMEM((pieces, group, PIECE), jnp.float32),
+            pltpu.VMEM((group, PIECE), jnp.float32),
             pltpu.VMEM((blk_n, group, 2 * HD), jnp.bfloat16),
             pltpu.VMEM((group, query_cols), jnp.bfloat16),
             pltpu.VMEM((group, query_cols), jnp.bfloat16),
@@ -507,8 +535,8 @@
             pltpu.SemaphoreType.DMA((pieces, chunks)),
             pltpu.SemaphoreType.DMA((3, chunks)),
             pltpu.SemaphoreType.DMA((3, chunks)),
-            pltpu.SemaphoreType.DMA((blk_n,)),
-            pltpu.SemaphoreType.DMA((blk_n,)),
+            pltpu.SemaphoreType.DMA((2, blk_n)),
+            pltpu.SemaphoreType.DMA((2, blk_n)),
             pltpu.SemaphoreType.DMA((uly_n,)),
             pltpu.SemaphoreType.DMA((uly_n,)),
         ],
@@ -533,7 +561,7 @@
     group_rows = tokens * uly_size
     tiles = group_rows // MBLK
     dp_n, blk_n = lax.axis_size("dp"), lax.axis_size("blk")
-    if dp_n == 2 and blk_n == 4 and uly_size == 4 and repeats == 1 and query_cols % PIECE == 0:
+    if dp_n == 2 and blk_n == 4 and uly_size == 4 and repeats == 1 and query_cols == 2 * PIECE and tokens * 2 == MBLK:
         positions = blk_rank * group_rows + jnp.arange(group_rows, dtype=jnp.int32)
         cosine, sine = angle_tables(positions)
         merged = fused(

time: 143 us -> 132 us (0.923)
  Pallas kernels: 139 us -> 128 us
    pallas_call x1, Pallas kernels: 139 us -> 128 us  [fused(): pl.pallas_call(functools.partial(fused_kernel, dp_n, blk_n), out_shape=ja...]
where the time goes in v3:
time: 132 us; the launch traced here: 131 us
  Pallas kernels  128 us (97%)
  other arithmetic  2.25 us (2%)
    pallas_call x1, Pallas kernels, fused(): pl.pallas_call(functools.partial(fused_kernel, dp_n, blk_n), out_shape=ja...  128 us

profile of v3, /device:TPU:28, one launch (start us, length us, event | category | flops | bytes accessed | tf_op | source)
XLA Modules:
  0.0 131.3 jit_solution(7890818910803422213)
XLA Ops:
  0.0 0.0 copy-start
  0.0 0.0 copy-start.1
  0.0 0.0 copy-start.2
  0.1 0.0 copy-start.3
  0.1 1.9 %fusion = (f32[1024,64]{1,0:T(8,128)S(1)}, f32[1024,64]{1,0:T(8,128)S(1)}, f32[1024,64]{1,0:T(8,128)S(1)}) fusion(f32[64]{0:T(128)S(1)} %negate_power_fusion, f32[1024]{0:T(1024)S(1)} %add_convert_fusion), kind=kLoop, calls=%fused_computation.4 | loop fusion | flops 131072 | bytes 790784 | tf_op jit(solution)/shard_map/neg | solution.py:574
  2.0 0.3 pad_maximum_fusion
  2.3 0.0 copy-done
  2.3 0.0 copy-done.1
  2.3 0.0 copy-done.2
  2.4 0.0 copy-done.3
  2.4 127.9 %shard_map.55 = bf16[256,2048]{1,0:T(8,128)(2,1)S(1)} custom-call(s32[8,8]{1,0:T(8,128)S(1)} %bitcast.4, bf16[256,4096]{1,0:T(8,128)(2,1)} %bitcast.5, bf16[512,512]{1,0:T(8,128)(2,1)S(1)} %copy-done, bf16[512,128]{1,0:T(8,128)(2,1)S(1)} %copy-done.1, bf16[512,128]{1,0:T(8,128)(2,1)S(1)} %copy-done.2, f32[1024,128]{1,0:T(8,128)S(1)} %get-tuple-element.8.cos_ref, ...), custom_call_target="tpu_custom_call" | custom-call | flops 6442450944 | bytes 8000000 | tf_op jit(solution)/shard_map/pallas_call | solution.py:518
  130.3 1.0 copy.7
  (2 shorter events, 0.0 us)
Async XLA Ops:
  0.0 2.3 %copy-start = (bf16[512,512]{1,0:T(8,128)(2,1)S(1)}, bf16[512,512]{1,0:T(8,128)(2,1)}, u32[]{:S(2)}) copy-start(bf16[512,512]{1,0:T(8,128)(2,1)} %wq.1) | copy-start | bytes 1572868
  0.0 2.3 %copy-start.1 = (bf16[512,128]{1,0:T(8,128)(2,1)S(1)}, bf16[512,128]{1,0:T(8,128)(2,1)}, u32[]{:S(2)}) copy-start(bf16[512,128]{1,0:T(8,128)(2,1)} %wk.1) | copy-start | bytes 393220
  0.0 2.3 %copy-start.2 = (bf16[512,128]{1,0:T(8,128)(2,1)S(1)}, bf16[512,128]{1,0:T(8,128)(2,1)}, u32[]{:S(2)}) copy-start(bf16[512,128]{1,0:T(8,128)(2,1)} %wv.1) | copy-start | bytes 393220
  0.1 2.3 %copy-start.3 = (s32[1,8,8]{2,1,0:T(8,128)S(1)}, s32[1,8,8]{2,1,0:T(8,128)}, u32[]{:S(2)}) copy-start(s32[1,8,8]{2,1,0:T(8,128)} %param.6) | copy-start | bytes 772

commit v4 on v3

--- a/solution.py
+++ b/solution.py
@@ -2,6 +2,7 @@
 
 import jax
 import jax.numpy as jnp
+import numpy as np
 from jax import lax
 from jax.experimental import pallas as pl
 from jax.experimental.pallas import tpu as pltpu
@@ -27,6 +28,14 @@
     frequency = jnp.power(jnp.float32(THETA_BASE), -exponent)
     angles = positions.astype(jnp.float32)[:, None] * frequency[None, :]
     return jnp.cos(angles), jnp.sin(angles)
+
+
+def turn_table(count):
+    exponent = np.arange(HD // 2, dtype=np.float32) * np.float32(2.0 / HD)
+    frequency = np.power(np.float32(THETA_BASE), -exponent)
+    angles = np.arange(count, dtype=np.float32)[:, None] * frequency[None, :]
+    cosine, sine = np.cos(angles), np.sin(angles)
+    return np.concatenate([cosine, cosine, -sine, sine], axis=1).astype(np.float32)
 
 
 def rotate(values, cosine, sine):
@@ -111,8 +120,8 @@
 
 
 def fused_kernel(
-    dp_n, blk_n, table, hid, wq, wk, wv, cos_ref, sin_ref, out,
-    weights, rows_all, acc, kv, q_rows, done, best, total, accum,
+    dp_n, blk_n, table, hid, wq, wk, wv, angles, out,
+    weights, rows_all, turns, acc, kv, q_rows, done, best, total, accum,
     local_sem, w_send, w_recv, h_send, h_recv, kv_send, kv_recv, o_send, o_recv,
 ):
     y, z, u = lax.axis_index("dp"), lax.axis_index("blk"), lax.axis_index("uly")
@@ -127,6 +136,7 @@
     chip = (u + 2) % 4
     far = (core + 2) % 4
     mine = y * blk_n + z
+    scale = HD**-0.5 * LOG2E
 
     barrier = pltpu.get_barrier_semaphore()
 
@@ -159,8 +169,12 @@
                 local_sem.at[pieces + 1 + c],
             )
         )
+    turn_copy = pltpu.make_async_copy(
+        angles.at[pl.ds(pl.multiple_of(z * group, group), group)], turns, local_sem.at[pieces + 1 + chunks]
+    )
     for copy in own:
         copy.start()
+    turn_copy.start()
     middle = jnp.where((z > 0) & (z < last), 1, 0)
     pl.semaphore_wait(barrier, 5 + middle)
 
@@ -261,7 +275,7 @@
         return result
 
     def turn(values, at):
-        return values * cos_ref[at, :] + pltpu.roll(values, HD // 2, 1) * sin_ref[at, :]
+        return values * turns[at, :HD] + pltpu.roll(values, HD // 2, 1) * turns[at, HD:]
 
     def kv_half(half):
         @pl.loop(0, MBLK // PIECE)
@@ -279,7 +293,7 @@
         for half in range(PIECE // HD):
             col = (p - 1) * PIECE + half * HD
             turned = turn(values[:, half * HD : (half + 1) * HD], at)
-            q_rows[at, col : col + HD] = turned.astype(jnp.bfloat16)
+            q_rows[at, col : col + HD] = (turned * scale).astype(jnp.bfloat16)
 
     def whole_queries(lower, upper):
         @pl.loop(lower, upper)
@@ -333,6 +347,119 @@
     for p in range(1, pieces):
         own[p + 1].wait()
     acc[...] = jnp.zeros_like(acc)
+    turn_copy.wait()
+
+    tiles = group // MBLK
+    query_cols = q_rows.shape[1]
+    pair_heads = PIECE // HD
+
+    def allowance(q_tile, source_z, k_tile):
+        allowed = table[z * tiles + q_tile, source_z * tiles + k_tile]
+        return jnp.where(allowed > 0, 0.0, -1e30).astype(jnp.float32)
+
+    def visit(pair, q_tile, source_z, k_tiles, first):
+        q_at = pl.ds(pl.multiple_of(q_tile * MBLK, MBLK), MBLK)
+        parts = [
+            kv.at[source_z, pl.ds(pl.multiple_of(k_tile * MBLK, MBLK), MBLK)] for k_tile in k_tiles
+        ]
+        biases = [0.0 if first else allowance(q_tile, source_z, k_tile) for k_tile in k_tiles]
+        for head in range(pair * pair_heads, (pair + 1) * pair_heads):
+            cols = slice(head * MBLK, (head + 1) * MBLK)
+            query = q_rows[q_at, head * HD : (head + 1) * HD]
+            all_scores = []
+            new_best = None if first else best[q_tile, :, cols]
+            old_best = new_best
+            for part, bias in zip(parts, biases):
+                scores = lax.dot_general(part[:, :HD], query, NT, preferred_element_type=jnp.float32)
+                if first:
+                    key_at = lax.broadcasted_iota(jnp.int32, (MBLK, MBLK), 0)
+                    query_at = lax.broadcasted_iota(jnp.int32, (MBLK, MBLK), 1)
+                    scores = jnp.where(key_at <= query_at, scores, -1e30)
+                    new_best = jnp.max(scores, axis=0, keepdims=True)
+                else:
+                    new_best = jnp.maximum(new_best, jnp.max(scores, axis=0, keepdims=True) + bias)
+                all_scores.append(scores)
+            sums, mixed = 0.0, 0.0
+            for part, bias, scores in zip(parts, biases, all_scores):
+                grown = jnp.exp2(scores - (new_best - bias))
+                sums += jnp.sum(grown, axis=0, keepdims=True)
+                mixed += lax.dot_general(
+                    part[:, HD:], grown.astype(jnp.bfloat16), TN, preferred_element_type=jnp.float32
+                )
+            best[q_tile, :, cols] = new_best
+            if first:
+                total[q_tile, :, cols] = sums
+                accum[q_tile, :, cols] = mixed
+            else:
+                rescale = jnp.exp2(old_best - new_best)
+                total[q_tile, :, cols] = total[q_tile, :, cols] * rescale + sums
+                accum[q_tile, :, cols] = accum[q_tile, :, cols] * rescale + mixed
+
+    def out_part(source, pair):
+        start = pl.multiple_of(source * query_cols + pair * PIECE, PIECE)
+        return out.at[:, pl.ds(start, PIECE)]
+
+    def done_part(owner, pair):
+        return done.at[pl.ds(owner * tokens, tokens), pl.ds(pair * PIECE, PIECE)]
+
+    def out_copy(owner, pair):
+        return pltpu.make_async_remote_copy(
+            src_ref=done_part(owner, pair), dst_ref=out_part(u, pair),
+            send_sem=o_send.at[pair, owner], recv_sem=o_recv.at[pair, u],
+            device_id={"uly": owner}, device_id_type=MESH,
+        )
+
+    def out_arrival(source, pair):
+        return pltpu.make_async_remote_copy(
+            src_ref=done_part(source, pair), dst_ref=out_part(source, pair),
+            send_sem=o_send.at[pair, source], recv_sem=o_recv.at[pair, source],
+            device_id={"uly": source}, device_id_type=MESH,
+        )
+
+    def out_own(pair):
+        return pltpu.make_async_copy(done_part(u, pair), out_part(u, pair), local_sem.at[pair])
+
+    def finalize(pair, q_tile):
+        q_at = pl.ds(pl.multiple_of(q_tile * MBLK, MBLK), MBLK)
+        for head in range(pair * pair_heads, (pair + 1) * pair_heads):
+            cols = slice(head * MBLK, (head + 1) * MBLK)
+            final = accum[q_tile, :, cols] / total[q_tile, :, cols]
+            done[q_at, head * HD : (head + 1) * HD] = final.T.astype(jnp.bfloat16)
+        owners = MBLK // tokens
+        for e in range(owners):
+            owner = q_tile * owners + e
+
+            @pl.when(owner != u)
+            def _():
+                out_copy(owner, pair).start()
+
+            @pl.when(owner == u)
+            def _():
+                out_own(pair).start()
+
+    def attend_own(pair):
+        @pl.loop(0, tiles)
+        def _(q_tile):
+            visit(pair, q_tile, z, [q_tile], True)
+
+            @pl.loop(0, q_tile)
+            def _(k_tile):
+                visit(pair, q_tile, z, [k_tile], False)
+
+            @pl.when(z == 0)
+            def _():
+                finalize(pair, q_tile)
+
+    def attend_lower(pair, d):
+        @pl.when(z >= d)
+        def _():
+            @pl.loop(0, tiles)
+            def _(q_tile):
+                visit(pair, q_tile, z - d, list(range(tiles)), False)
+
+                @pl.when(z == d)
+                def _():
+                    finalize(pair, q_tile)
 
     slabs = group // PIECE
     ends = (0, 1, 3, 5, 7, 8)
@@ -362,12 +489,13 @@
                 kv_pass(1, 1)
                 for e in range(blk_n):
                     across_arrived(1, e)
-                whole_queries(0, slabs // 2)
+                whole_queries(0, slabs)
                 query_chunks(1)
             elif step == 8:
-                whole_queries(slabs // 2, slabs)
+                attend_own(0)
                 query_chunks(2)
                 kv_pass(2, 1)
+                attend_lower(0, 1)
                 query_chunks(3)
             step += 1
 
@@ -376,113 +504,14 @@
         at = pl.ds(pl.multiple_of(i * PIECE, PIECE), PIECE)
         keep_query(pieces - 1, at, acc[at, :])
 
-    scale = HD**-0.5 * LOG2E
-    tiles = group // MBLK
-    heads = q_rows.shape[1] // HD
-    query_cols = q_rows.shape[1]
-
-    def visit(q_tile, source_z, k_tile, first):
-        keys = kv.at[source_z, pl.ds(pl.multiple_of(k_tile * MBLK, MBLK), MBLK)]
-        key, value = keys[:, :HD], keys[:, HD:]
-        q_at = pl.ds(pl.multiple_of(q_tile * MBLK, MBLK), MBLK)
-        allowed = table[z * tiles + q_tile, source_z * tiles + k_tile]
-        bias = jnp.where(allowed > 0, 0.0, -1e30).astype(jnp.float32)
-        for head in range(heads):
-            cols = slice(head * MBLK, (head + 1) * MBLK)
-            query = q_rows[q_at, head * HD : (head + 1) * HD]
-            scores = lax.dot_general(key, query, NT, preferred_element_type=jnp.float32) * scale
-            if first:
-                key_at = lax.broadcasted_iota(jnp.int32, (MBLK, MBLK), 0)
-                query_at = lax.broadcasted_iota(jnp.int32, (MBLK, MBLK), 1)
-                scores = jnp.where(key_at <= query_at, scores, -1e30)
-                new_best = jnp.max(scores, axis=0, keepdims=True)
-            else:
-                scores = scores + bias
-                old_best = best[q_tile, :, cols]
-                new_best = jnp.maximum(old_best, jnp.max(scores, axis=0, keepdims=True))
-            grown = jnp.exp2(scores - new_best)
-            sums = jnp.sum(grown, axis=0, keepdims=True)
-            mixed = lax.dot_general(
-                value, grown.astype(jnp.bfloat16), TN, preferred_element_type=jnp.float32
-            )
-            best[q_tile, :, cols] = new_best
-            if first:
-                total[q_tile, :, cols] = sums
-                accum[q_tile, :, cols] = mixed
-            else:
-                rescale = jnp.exp2(old_best - new_best)
-                total[q_tile, :, cols] = total[q_tile, :, cols] * rescale + sums
-                accum[q_tile, :, cols] = accum[q_tile, :, cols] * rescale + mixed
-
-    def out_copy(owner):
-        return pltpu.make_async_remote_copy(
-            src_ref=done.at[pl.ds(owner * tokens, tokens)],
-            dst_ref=out.at[:, pl.ds(pl.multiple_of(u * query_cols, query_cols), query_cols)],
-            send_sem=o_send.at[owner], recv_sem=o_recv.at[u],
-            device_id={"uly": owner}, device_id_type=MESH,
-        )
-
-    def out_arrival(source):
-        return pltpu.make_async_remote_copy(
-            src_ref=done.at[pl.ds(source * tokens, tokens)],
-            dst_ref=out.at[:, pl.ds(pl.multiple_of(source * query_cols, query_cols), query_cols)],
-            send_sem=o_send.at[source], recv_sem=o_recv.at[source],
-            device_id={"uly": source}, device_id_type=MESH,
-        )
-
-    def out_own():
-        return pltpu.make_async_copy(
-            done.at[pl.ds(u * tokens, tokens)],
-            out.at[:, pl.ds(pl.multiple_of(u * query_cols, query_cols), query_cols)],
-            local_sem.at[0],
-        )
-
-    def finalize(q_tile):
-        q_at = pl.ds(pl.multiple_of(q_tile * MBLK, MBLK), MBLK)
-        for head in range(heads):
-            cols = slice(head * MBLK, (head + 1) * MBLK)
-            final = accum[q_tile, :, cols] / total[q_tile, :, cols]
-            done[q_at, head * HD : (head + 1) * HD] = final.T.astype(jnp.bfloat16)
-        owners = MBLK // tokens
-        for e in range(owners):
-            owner = q_tile * owners + e
-
-            @pl.when(owner != u)
-            def _():
-                out_copy(owner).start()
-
-            @pl.when(owner == u)
-            def _():
-                out_own().start()
-
-    @pl.loop(0, tiles)
-    def _(q_tile):
-        visit(q_tile, z, q_tile, True)
-
-        @pl.loop(0, q_tile)
-        def _(k_tile):
-            visit(q_tile, z, k_tile, False)
-
-        @pl.when(z == 0)
-        def _():
-            finalize(q_tile)
-
-    for d in range(1, blk_n):
-        if d == last:
-            kv_pass(d, 0)
-            kv_pass(d, 1)
-
-        @pl.when(z >= d)
-        def _(d=d):
-            @pl.loop(0, tiles)
-            def _(q_tile):
-                @pl.loop(0, tiles)
-                def _(k_tile):
-                    visit(q_tile, z - d, k_tile, False)
-
-                @pl.when(z == d)
-                def _():
-                    finalize(q_tile)
+    attend_lower(0, 2)
+    attend_own(1)
+    attend_lower(1, 1)
+    kv_pass(3, 0)
+    kv_pass(3, 1)
+    attend_lower(0, 3)
+    attend_lower(1, 2)
+    attend_lower(1, 3)
 
     for p in range(pieces):
         own_weights(p, finish=True)
@@ -500,13 +529,14 @@
                 kv_copy(e, 0).wait_send()
                 kv_copy(e, 1).wait_send()
 
-    out_own().wait()
-    for other in (core, chip, far):
-        out_copy(other).wait_send()
-        out_arrival(other).wait_recv()
-
-
-def fused(table, hid, wq, wk, wv, cosine, sine, dp_n, blk_n, uly_n):
+    for pair in range(pieces - 1):
+        out_own(pair).wait()
+        for other in (core, chip, far):
+            out_copy(other, pair).wait_send()
+            out_arrival(other, pair).wait_recv()
+
+
+def fused(table, hid, wq, wk, wv, angles, dp_n, blk_n, uly_n):
     tokens, width = hid.shape
     depth, query_cols = wq.shape
     chunks = dp_n * blk_n
@@ -514,15 +544,15 @@
     pieces = 1 + query_cols // PIECE
     tiles, heads = group // MBLK, query_cols // HD
     hbm = pl.BlockSpec(memory_space=pl.ANY)
-    vmem = pl.BlockSpec(memory_space=pltpu.VMEM)
     return pl.pallas_call(
         functools.partial(fused_kernel, dp_n, blk_n),
         out_shape=jax.ShapeDtypeStruct((tokens, uly_n * query_cols), jnp.bfloat16),
-        in_specs=[pl.BlockSpec(memory_space=pltpu.SMEM), hbm, hbm, hbm, hbm, vmem, vmem],
+        in_specs=[pl.BlockSpec(memory_space=pltpu.SMEM), hbm, hbm, hbm, hbm, hbm],
         out_specs=hbm,
         scratch_shapes=[
             pltpu.VMEM((pieces, chunks, depth, PIECE), jnp.bfloat16),
             pltpu.VMEM((chunks, group, depth), jnp.bfloat16),
+            pltpu.VMEM((group, 2 * HD), jnp.float32),
             pltpu.VMEM((group, PIECE), jnp.float32),
             pltpu.VMEM((blk_n, group, 2 * HD), jnp.bfloat16),
             pltpu.VMEM((group, query_cols), jnp.bfloat16),
@@ -530,15 +560,15 @@
             pltpu.VMEM((tiles, 1, heads * MBLK), jnp.float32),
             pltpu.VMEM((tiles, 1, heads * MBLK), jnp.float32),
             pltpu.VMEM((tiles, HD, heads * MBLK), jnp.float32),
-            pltpu.SemaphoreType.DMA((pieces + 1 + chunks,)),
+            pltpu.SemaphoreType.DMA((pieces + 2 + chunks,)),
             pltpu.SemaphoreType.DMA((pieces, 3, blk_n)),
             pltpu.SemaphoreType.DMA((pieces, chunks)),
             pltpu.SemaphoreType.DMA((3, chunks)),
             pltpu.SemaphoreType.DMA((3, chunks)),
             pltpu.SemaphoreType.DMA((2, blk_n)),
             pltpu.SemaphoreType.DMA((2, blk_n)),
-            pltpu.SemaphoreType.DMA((uly_n,)),
-            pltpu.SemaphoreType.DMA((uly_n,)),
+            pltpu.SemaphoreType.DMA((pieces - 1, uly_n)),
+            pltpu.SemaphoreType.DMA((pieces - 1, uly_n)),
         ],
         compiler_params=pltpu.CompilerParams(
             collective_id=0, has_side_effects=True, vmem_limit_bytes=50 * 1024 * 1024
@@ -546,7 +576,7 @@
         cost_estimate=pl.CostEstimate(
             flops=2 * group * width * (query_cols + 2 * HD), bytes_accessed=8 * 10**6, transcendentals=0
         ),
-    )(table, hid, wq, wk, wv, cosine, sine)
+    )(table, hid, wq, wk, wv, angles)
 
 
 def shards(hidden_states, block_table, w_query, w_key, w_value):
@@ -562,16 +592,13 @@
     tiles = group_rows // MBLK
     dp_n, blk_n = lax.axis_size("dp"), lax.axis_size("blk")
     if dp_n == 2 and blk_n == 4 and uly_size == 4 and repeats == 1 and query_cols == 2 * PIECE and tokens * 2 == MBLK:
-        positions = blk_rank * group_rows + jnp.arange(group_rows, dtype=jnp.int32)
-        cosine, sine = angle_tables(positions)
         merged = fused(
             block_table[0],
             hidden_states[0],
             w_query,
             w_key,
             w_value,
-            jnp.concatenate([cosine, cosine], axis=1),
-            jnp.concatenate([-sine, sine], axis=1),
+            jnp.asarray(turn_table(blk_n * group_rows)),
             dp_n,
             blk_n,
             uly_size,

time: 132 us -> 127 us (0.962)
  Pallas kernels: 128 us -> 119 us
  local copies, waits for them, and re-layouts: 1 us -> 6.1 us
  other arithmetic: 2.25 us -> 0 us
    pallas_call x1, Pallas kernels: 128 us -> 119 us  [fused(): pl.pallas_call(functools.partial(fused_kernel, dp_n, blk_n), out_shape=ja...]
    unnamed x9 -> x11, local copies, waits for them, and re-layouts: 1 us -> 6.1 us
    neg x1 -> x0, other arithmetic: 1.9 us -> none  [shards(): -sine]
where the time goes in v4:
time: 127 us; the launch traced here: 125 us
  Pallas kernels  119 us (94%)
  local copies, waits for them, and re-layouts  6.1 us (5%)
    pallas_call x1, Pallas kernels, fused(): pl.pallas_call(functools.partial(fused_kernel, dp_n, blk_n), out_shape=ja...  119 us
    unnamed x11, local copies, waits for them, and re-layouts  6.1 us

profile of v4, /device:TPU:28, one launch (start us, length us, event | category | flops | bytes accessed | tf_op | source)
XLA Modules:
  0.0 125.5 jit_solution(4112512703250112585)
XLA Ops:
  0.0 0.0 copy-start
  0.0 1.6 %copy-done = bf16[1,256,4096]{2,1,0:T(8,128)(2,1)S(1)} copy-done((bf16[1,256,4096]{2,1,0:T(8,128)(2,1)S(1)}, bf16[1,256,4096]{2,1,0:T(8,128)(2,1)}, u32[]{:S(2)}) %copy-start) | copy-done | bytes 2097176
  1.6 0.0 copy-start.1
  1.6 1.0 copy-done.1
  2.6 0.0 copy-start.2
  2.6 0.9 copy-done.2
  3.5 0.0 copy-start.3
  3.5 0.9 copy-done.3
  4.4 0.0 copy-start.4
  4.4 0.7 copy-done.4
  5.1 119.4 %shard_map.64 = bf16[256,2048]{1,0:T(8,128)(2,1)S(1)} custom-call(s32[8,8]{1,0:T(8,128)S(1)} %bitcast.5, bf16[256,4096]{1,0:T(8,128)(2,1)S(1)} %bitcast.4, bf16[512,512]{1,0:T(8,128)(2,1)S(1)} %copy-done.1, bf16[512,128]{1,0:T(8,128)(2,1)S(1)} %copy-done.2, bf16[512,128]{1,0:T(8,128)(2,1)S(1)} %copy-done.3, f32[4096,256]{1,0:T(8,128)} %constant.2.clone.angles), custom_call_target="tpu_custom_call" | custom-call | flops 6442450944 | bytes 8000000 | tf_op jit(solution)/shard_map/pallas_call | solution.py:547
  124.5 1.0 copy.8
Async XLA Ops:
  0.0 1.6 %copy-start = (bf16[1,256,4096]{2,1,0:T(8,128)(2,1)S(1)}, bf16[1,256,4096]{2,1,0:T(8,128)(2,1)}, u32[]{:S(2)}) copy-start(bf16[1,256,4096]{2,1,0:T(8,128)(2,1)} %param.6) | copy-start | bytes 6291460
  1.6 1.0 copy-start.1
  2.6 0.9 copy-start.2
  3.5 0.9 copy-start.3
  4.4 0.7 copy-start.4

commit v5 on v4

--- a/solution.py
+++ b/solution.py
@@ -140,14 +140,10 @@
 
     barrier = pltpu.get_barrier_semaphore()
 
-    @pl.when(z < last)
-    def _():
-        pl.semaphore_signal(barrier, inc=1, device_id=up, device_id_type=MESH)
-
-    @pl.when(z > 0)
-    def _():
-        pl.semaphore_signal(barrier, inc=1, device_id=down, device_id_type=MESH)
-
+    for k in range(1, blk_n):
+        pl.semaphore_signal(
+            barrier, inc=1, device_id={"blk": lax.rem(z + k, blk_n)}, device_id_type=MESH
+        )
     for where in (across, {"uly": core}, {"uly": chip}, {"uly": far}):
         pl.semaphore_signal(barrier, inc=1, device_id=where, device_id_type=MESH)
 
@@ -175,8 +171,7 @@
     for copy in own:
         copy.start()
     turn_copy.start()
-    middle = jnp.where((z > 0) & (z < last), 1, 0)
-    pl.semaphore_wait(barrier, 5 + middle)
+    pl.semaphore_wait(barrier, blk_n + 3)
 
     def weight_copy(p, way, source_z, where, rank):
         return pltpu.make_async_remote_copy(
@@ -198,12 +193,12 @@
         tile = own_tile if half == 0 else 1 - own_tile
         return pl.multiple_of(tile * MBLK, MBLK)
 
-    def kv_copy(source_z, half):
+    def kv_copy(source_z, half, target):
         part = kv.at[source_z, pl.ds(tile_rows(half), MBLK)]
         return pltpu.make_async_remote_copy(
             src_ref=part, dst_ref=part,
-            send_sem=kv_send.at[half, source_z], recv_sem=kv_recv.at[half, source_z],
-            device_id=up, device_id_type=MESH,
+            send_sem=kv_send.at[half, target], recv_sem=kv_recv.at[half, source_z],
+            device_id={"blk": target}, device_id_type=MESH,
         )
 
     def own_weights(p, finish=False):
@@ -285,9 +280,10 @@
             kv[z, at, :HD] = turn(both[:, :HD], at).astype(jnp.bfloat16)
             kv[z, at, HD:] = both[:, HD:].astype(jnp.bfloat16)
 
-        @pl.when(z < last)
-        def _():
-            kv_copy(z, half).start()
+        for t in range(1, blk_n):
+            @pl.when(z + t <= last)
+            def _(t=t):
+                kv_copy(z, half, z + t).start()
 
     def keep_query(p, at, values):
         for half in range(PIECE // HD):
@@ -319,14 +315,11 @@
             multiply(y * blk_n + z + d)
             multiply((1 - y) * blk_n + z + d)
 
-    def kv_pass(d, half):
+    def kv_arrived(d):
         @pl.when(z >= d)
         def _():
-            kv_copy(z - d, half).wait_recv()
-
-            @pl.when(z < last)
-            def _():
-                kv_copy(z - d, half).start()
+            for half in range(2):
+                kv_copy(z - d, half, z - d).wait_recv()
 
     def hidden_step(lower, upper):
         for c in range(lower, upper):
@@ -478,15 +471,12 @@
                     hidden_copy(0, c, core, core).wait_recv()
                 kv_half(0)
             elif step == 5:
-                kv_pass(1, 0)
                 for c in range(chunks):
                     hidden_copy(2, c, far, core).wait_recv()
                 kv_half(1)
             elif step == 6:
                 query_chunks(0)
             elif step == 7:
-                kv_pass(2, 0)
-                kv_pass(1, 1)
                 for e in range(blk_n):
                     across_arrived(1, e)
                 whole_queries(0, slabs)
@@ -494,7 +484,7 @@
             elif step == 8:
                 attend_own(0)
                 query_chunks(2)
-                kv_pass(2, 1)
+                kv_arrived(1)
                 attend_lower(0, 1)
                 query_chunks(3)
             step += 1
@@ -504,11 +494,11 @@
         at = pl.ds(pl.multiple_of(i * PIECE, PIECE), PIECE)
         keep_query(pieces - 1, at, acc[at, :])
 
+    kv_arrived(2)
     attend_lower(0, 2)
     attend_own(1)
     attend_lower(1, 1)
-    kv_pass(3, 0)
-    kv_pass(3, 1)
+    kv_arrived(3)
     attend_lower(0, 3)
     attend_lower(1, 2)
     attend_lower(1, 3)
@@ -521,13 +511,11 @@
         hidden_copy(0, c, u, core).wait_send()
         hidden_copy(1, c, u, chip).wait_send()
         hidden_copy(2, c, chip, core).wait_send()
-    for e in range(blk_n):
-        @pl.when(e <= z)
-        def _(e=e):
-            @pl.when(z < last)
-            def _():
-                kv_copy(e, 0).wait_send()
-                kv_copy(e, 1).wait_send()
+    for t in range(1, blk_n):
+        @pl.when(z + t <= last)
+        def _(t=t):
+            for half in range(2):
+                kv_copy(z, half, z + t).wait_send()
 
     for pair in range(pieces - 1):
         out_own(pair).wait()
@@ -571,7 +559,7 @@
             pltpu.SemaphoreType.DMA((pieces - 1, uly_n)),
         ],
         compiler_params=pltpu.CompilerParams(
-            collective_id=0, has_side_effects=True, vmem_limit_bytes=50 * 1024 * 1024
+            collective_id=0, has_side_effects=True, vmem_limit_bytes=60 * 1024 * 1024
         ),
         cost_estimate=pl.CostEstimate(
             flops=2 * group * width * (query_cols + 2 * HD), bytes_accessed=8 * 10**6, transcendentals=0

time: 127 us -> 132 us (1.039)
  Pallas kernels: 119 us -> 129 us
  local copies, waits for them, and re-layouts: 6.1 us -> 2.3 us
    pallas_call x1, Pallas kernels: 119 us -> 129 us  [fused(): pl.pallas_call(functools.partial(fused_kernel, dp_n, blk_n), out_shape=ja...]
    unnamed x11 -> x1, local copies, waits for them, and re-layouts: 6.1 us -> 2.3 us
where the time goes in v5:
time: 132 us; the launch traced here: 131 us
  Pallas kernels  129 us (98%)
  local copies, waits for them, and re-layouts  2.3 us (2%)
    pallas_call x1, Pallas kernels, fused(): pl.pallas_call(functools.partial(fused_kernel, dp_n, blk_n), out_shape=ja...  129 us

profile of v5, /device:TPU:28, one launch (start us, length us, event | category | flops | bytes accessed | tf_op | source)
XLA Modules:
  0.0 131.2 jit_solution(3231964210552510679)
XLA Ops:
  0.0 128.9 %shard_map.64 = bf16[256,2048]{1,0:T(8,128)(2,1)} custom-call(s32[8,8]{1,0:T(8,128)} %bitcast.5, bf16[256,4096]{1,0:T(8,128)(2,1)} %bitcast.4, bf16[512,512]{1,0:T(8,128)(2,1)} %wq.1, bf16[512,128]{1,0:T(8,128)(2,1)} %wk.1, bf16[512,128]{1,0:T(8,128)(2,1)} %wv.1, f32[4096,256]{1,0:T(8,128)} %constant.2.clone.angles), custom_call_target="tpu_custom_call" | custom-call | flops 6442450944 | bytes 8000000 | tf_op jit(solution)/shard_map/pallas_call | solution.py:535
  128.9 2.3 %copy.8 = bf16[1,256,2048]{2,1,0:T(8,128)(2,1)} copy(bf16[1,256,2048]{2,1,0:T(8,128)(2,1)} %bitcast.3) | data formatting | bytes 2097152

commit v6 on v4

--- a/solution.py
+++ b/solution.py
@@ -493,8 +493,8 @@
                 query_chunks(1)
             elif step == 8:
                 attend_own(0)
+                kv_pass(2, 1)
                 query_chunks(2)
-                kv_pass(2, 1)
                 attend_lower(0, 1)
                 query_chunks(3)
             step += 1
@@ -571,7 +571,7 @@
             pltpu.SemaphoreType.DMA((pieces - 1, uly_n)),
         ],
         compiler_params=pltpu.CompilerParams(
-            collective_id=0, has_side_effects=True, vmem_limit_bytes=50 * 1024 * 1024
+            collective_id=0, has_side_effects=True, vmem_limit_bytes=60 * 1024 * 1024
         ),
         cost_estimate=pl.CostEstimate(
             flops=2 * group * width * (query_cols + 2 * HD), bytes_accessed=8 * 10**6, transcendentals=0

time: 127 us -> 125 us (0.984)
  local copies, waits for them, and re-layouts: 6.1 us -> 2.3 us
  Pallas kernels: 119 us -> 121 us
    unnamed x11 -> x1, local copies, waits for them, and re-layouts: 6.1 us -> 2.3 us
    pallas_call x1, Pallas kernels: 119 us -> 121 us  [fused(): pl.pallas_call(functools.partial(fused_kernel, dp_n, blk_n), out_shape=ja...]
where the time goes in v6:
time: 125 us; the launch traced here: 124 us
  Pallas kernels  121 us (97%)
  local copies, waits for them, and re-layouts  2.3 us (2%)
    pallas_call x1, Pallas kernels, fused(): pl.pallas_call(functools.partial(fused_kernel, dp_n, blk_n), out_shape=ja...  121 us

profile of v6, /device:TPU:28, one launch (start us, length us, event | category | flops | bytes accessed | tf_op | source)
XLA Modules:
  0.0 123.6 jit_solution(5367877147874949311)
XLA Ops:
  0.0 121.3 %shard_map.64 = bf16[256,2048]{1,0:T(8,128)(2,1)} custom-call(s32[8,8]{1,0:T(8,128)} %bitcast.5, bf16[256,4096]{1,0:T(8,128)(2,1)} %bitcast.4, bf16[512,512]{1,0:T(8,128)(2,1)} %wq.1, bf16[512,128]{1,0:T(8,128)(2,1)} %wk.1, bf16[512,128]{1,0:T(8,128)(2,1)} %wv.1, f32[4096,256]{1,0:T(8,128)} %constant.2.clone.angles), custom_call_target="tpu_custom_call" | custom-call | flops 6442450944 | bytes 8000000 | tf_op jit(solution)/shard_map/pallas_call | solution.py:547
  121.3 2.3 %copy.8 = bf16[1,256,2048]{2,1,0:T(8,128)(2,1)} copy(bf16[1,256,2048]{2,1,0:T(8,128)(2,1)} %bitcast.3) | data formatting | bytes 2097152
